TPU v7x, 256 devices: a whole 4x4x8 slice. The times are simulated.
256 devices in a mesh: band: 32 (over z, y_lo, core), pw: 8 (over y_hi, x).
Axes of the slice: x: 4, y: 4 (y_hi: 2, y_lo: 2; y = y_hi * 2 + y_lo), z: 8, core: 2. Of those that a mesh axis runs over, the one named last changes fastest.
Arguments:
- elements: bfloat16 [64, 4096, 256], P('band', 'pw'), may hold values from -8 to 8
- strength: bfloat16 [4096, 4096], P('pw', 'band'), may hold values from -6 to 6
- pole_freq: bfloat16 [4096, 4096], P('pw', 'band'), may hold values from 0.5 to 4
- energies: float32 [64], P('band'), may hold values from -2 to 2
- imag_freqs: float32 [2], replicated, may hold values from 0.25 to 2
Outputs:
- sigma: float32 [2, 256, 256], P(None, 'band', 'pw')
All inputs are finite; a program needn't handle non-finite values.
Results may differ from a plain program's by a relative error of at most 0.006.
Values may be sent and summed in bfloat16 or wider, within the bound.
A program may use at most 64 MiB of HBM per device.

v0:
```python
import math

import jax
import jax.numpy as jnp
from jax import lax
from jax.sharding import PartitionSpec as P


def shifted_2(value, axis, steps):
    count = lax.axis_size(axis)
    pairs = [(source, (source + steps) % count) for source in range(count)]
    return lax.ppermute(value, axis, pairs)


def on_device(elements, strength, pole_freq, energies, imag_freqs):
    band_count, row_count, states = elements.shape
    column_count = strength.shape[1]
    half_rows = row_count // 2
    band_size = lax.axis_size("band")
    plane_size = lax.axis_size("pw")
    my_index = lax.axis_index("band")
    whole_rows = lax.all_gather(elements, "pw", axis=1, tiled=True)
    nu_square = imag_freqs * imag_freqs
    rows_split = elements.reshape(band_count, 2, half_rows, states)

    def contribute(running, screen, column_start):
        width = screen.shape[2]
        strength_f = screen[0].astype(jnp.float32)
        shifted = screen[1].astype(jnp.float32)[None] + energies[:, None, None]
        kernel = (
            strength_f[None, None]
            * shifted[None]
            / (nu_square[:, None, None, None] + shifted[None] * shifted[None])
        ).astype(jnp.bfloat16)
        kernel = kernel.reshape(2, band_count, 2, half_rows, width)
        partial_value = jnp.einsum(
            "bhgn,ebhgc->ebhnc", rows_split, kernel, preferred_element_type=jnp.float32
        ).astype(jnp.bfloat16)
        column_rows = lax.dynamic_slice_in_dim(whole_rows, jnp.asarray(column_start), width, 1)
        return running + jnp.einsum(
            "ebhnc,bcm->enm", partial_value, column_rows, preferred_element_type=jnp.float32
        )

    own_screen = jnp.stack((strength, pole_freq))
    empty = jnp.zeros((2, states, states), jnp.float32)
    running = contribute(empty, own_screen, my_index * column_count)

    def one_way(offset, carry):
        screen, summed = carry
        screen = shifted_2(screen, "band", 1)
        summed = contribute(summed, screen, (my_index - offset) % band_size * column_count)
        return (screen, summed)

    running = lax.fori_loop(1, band_size, one_way, (own_screen, running))[1]
    plane_total = row_count * plane_size
    scaled = running / (plane_total * math.sqrt(band_count * band_size))
    rows_each = states // band_size
    cols_each = states // plane_size
    blocks = scaled.reshape(2, band_size, rows_each, plane_size, cols_each).transpose(1, 3, 0, 2, 4)
    blocks = blocks.reshape(band_size * plane_size, 2, rows_each, cols_each)
    return lax.psum_scatter(blocks, ("band", "pw"), scatter_dimension=0, tiled=True)[0]


def solution(mesh):
    in_specs = (P("band", "pw", None), P("pw", "band"), P("pw", "band"), P("band"), P())
    out_specs = P(None, "band", "pw")
    return jax.shard_map(
        on_device, mesh=mesh, in_specs=in_specs, out_specs=out_specs, check_vma=False
    )
```

profile of v0, /device:TPU:1, one launch (start us, length us, event | category | flops | bytes accessed | tf_op | source)
XLA Modules:
  0.0 1664.7 jit_solution(4737424197970810751)
XLA Ops:
  11.8 1.5 fusion.10
  13.3 76.7 %all-gather.2.cloned.1.call-done = bf16[2,4096,256]{2,1,0:T(8,128)(2,1)} async-done(((bf16[2,512,256]{2,1,0:T(8,128)(2,1)}), bf16[2,4096,256]{2,1,0:T(8,128)(2,1)}) %all-gather.2.cloned.1.call-update) | async-done | bytes 4194320 | tf_op jit(solution)/shard_map/all_gather | solution.py:22
  91.2 301.8 %while.17 = (s32[]{:T(128)}, bf16[2,512,128]{2,1,0:T(8,128)(2,1)S(1)}, f32[2,256,256]{2,1,0:T(8,128)S(1)}, f32[2]{0:T(128)S(1)}, f32[2]{0:T(128)S(1)}, /*index=5...) while((s32[]{:T(128)}, ...), condition=%wide.region_3.4_spmd, body=%wide.region_1.3_spmd.sunk | while | flops 203423744 | bytes 7733608 | solution.py:54
  91.2 1.3 collective-permute-start
  92.6 3.3 collective-permute-done
  96.6 1.2 fusion.31
  97.8 2.6 collective-permute-start
  100.4 3.3 collective-permute-done
  104.4 1.2 fusion.31
  105.6 2.6 collective-permute-start
  108.2 5.1 collective-permute-done
  116.0 7.2 collective-permute-done
  123.9 1.2 fusion.31
  125.2 7.9 collective-permute-done
  133.8 1.2 fusion.31
  135.2 7.9 collective-permute-done
  143.7 1.2 fusion.31
  145.1 7.9 collective-permute-done
  153.7 1.2 fusion.31
  155.0 7.9 collective-permute-done
  163.6 1.2 fusion.31
  164.9 7.9 collective-permute-done
  173.5 1.2 fusion.31
  174.9 7.9 collective-permute-done
  184.8 7.9 collective-permute-done
  193.4 1.2 fusion.31
  194.7 7.9 collective-permute-done
  203.3 1.2 fusion.31
  204.6 7.9 collective-permute-done
  213.2 1.2 fusion.31
  214.6 7.9 collective-permute-done
  223.1 1.2 fusion.31
  224.5 7.9 collective-permute-done
  233.0 1.2 fusion.31
  234.4 7.9 collective-permute-done
  243.0 1.2 fusion.31
  244.3 7.9 collective-permute-done
  254.2 7.9 collective-permute-done
  262.8 1.2 fusion.31
  264.2 7.9 collective-permute-done
  272.7 1.2 fusion.31
  274.1 7.9 collective-permute-done
  282.7 1.2 fusion.31
  284.0 7.9 collective-permute-done
  292.6 1.2 fusion.31
  293.9 7.9 collective-permute-done
  302.5 1.2 fusion.31
  303.9 7.9 collective-permute-done
  312.4 1.2 fusion.31
  313.8 7.9 collective-permute-done
  323.7 7.9 collective-permute-done
  332.3 1.2 fusion.31
  333.6 7.9 collective-permute-done
  342.2 1.2 fusion.31
  343.6 7.9 collective-permute-done
  352.1 1.2 fusion.31
  353.5 7.9 collective-permute-done
  362.1 1.2 fusion.31
  363.4 7.9 collective-permute-done
  372.0 1.2 fusion.31
  373.3 7.9 collective-permute-done
  383.3 7.9 collective-permute-done
  393.6 1.7 copy.9
  395.3 1262.6 %reduce-scatter.2.cloned.1.call-done = f32[1,2,8,32]{3,2,1,0:T(8,128)} async-done(((f32[256,2,8,32]{3,2,1,0:T(8,128)}), f32[1,2,8,32]{3,2,1,0:T(8,128)}) %reduce-scatter.2.cloned.1.call-update) | async-done | bytes 2064 | tf_op jit(solution)/shard_map/reduce_scatter | solution.py:61
  (236 shorter events, 38.3 us)
Async XLA Ops:
  6.5 83.5 %all-gather.2.cloned.1.call-start = ((), (), s32[]{:S(2)}) async-start(), calls=%async_computation.1 | async-start | bytes 4718592 | tf_op jit(solution)/shard_map/all_gather | solution.py:22
  7.3 1650.6 %reduce-scatter.2.cloned.1.call-start = ((), (), s32[]{:S(2)}) async-start(), calls=%async_computation.2 | async-start | bytes 2105344 | tf_op jit(solution)/shard_map/reduce_scatter | solution.py:61
  9.0 82.2 %copy-start = (bf16[2,512,256]{2,1,0:T(8,128)(2,1)S(1)}, bf16[2,512,256]{2,1,0:T(8,128)(2,1)}, u32[]{:S(2)}) copy-start(bf16[2,512,256]{2,1,0:T(8,128)(2,1)} %param.7) | copy-start | bytes 1572868
  9.0 82.2 %copy-start.1 = (f32[2]{0:T(128)S(1)}, f32[2]{0:T(128)}, u32[]{:S(2)}) copy-start(f32[2]{0:T(128)} %param.10) | copy-start | bytes 28
  91.2 4.7 collective-permute-start
  97.8 5.9 collective-permute-start
  105.6 7.6 collective-permute-start
  115.2 8.0 collective-permute-start
  125.1 8.0 collective-permute-start
  135.1 8.0 collective-permute-start
  145.0 8.0 collective-permute-start
  154.9 8.0 collective-permute-start
  164.8 8.0 collective-permute-start
  174.7 8.0 collective-permute-start
  184.7 8.0 collective-permute-start
  194.6 8.0 collective-permute-start
  204.5 8.0 collective-permute-start
  214.4 8.0 collective-permute-start
  224.4 8.0 collective-permute-start
  234.3 8.0 collective-permute-start
  244.2 8.0 collective-permute-start
  254.1 8.0 collective-permute-start
  264.1 8.0 collective-permute-start
  274.0 8.0 collective-permute-start
  283.9 8.0 collective-permute-start
  293.8 8.0 collective-permute-start
  303.8 8.0 collective-permute-start
  313.7 8.0 collective-permute-start
  323.6 8.0 collective-permute-start
  333.5 8.0 collective-permute-start
  343.4 8.0 collective-permute-start
  353.4 8.0 collective-permute-start
  363.3 8.0 collective-permute-start
  373.2 8.0 collective-permute-start
  383.1 8.0 collective-permute-start
Sparse Core Ops, SparseCore 0:
  10.0 79.9 all-gather.1
  395.4 1262.4 reduce-scatter.1
where the time goes:
time: 1680 us; the launch traced here: 1660 us
  waiting for transfers between devices  1570 us (93%)
  matrix products  53.9 us (3%)
    reduce_scatter x1, waiting for transfers between devices, on_device(): lax.psum_scatter(blocks, ('band', 'pw'), scatter_dimension=0, tiled=True)[0]  1260 us
    ppermute x31, waiting for transfers between devices, shifted_2(): return lax.ppermute(value, axis, pairs)  231 us
    all_gather x1, waiting for transfers between devices, on_device(): whole_rows = lax.all_gather(elements, 'pw', axis=1, tiled=True)  76.7 us
    dot_general x32, matrix products, contribute(): jnp.einsum('ebhnc,bcm->enm', partial_value, column_rows, preferred_elemen...  38.2 us
  transfers between devices with their start and end apart: 33, of which 33 were waited for; matrix products, arithmetic and copies ran while one was open for 0% of the time, Pallas kernels for 0%

commit v1 on v0

v1 whole, which is shorter than its diff:
```python
import math

import jax
import jax.numpy as jnp
from jax import lax
from jax.experimental import pallas as pl
from jax.experimental.pallas import tpu as pltpu
from jax.sharding import PartitionSpec as P

MESH = pl.DeviceIdType.MESH
XS, YS, ZS = 4, 4, 8
BF = jnp.bfloat16
F32 = jnp.float32


def body(scale, e_ref, s_ref, w_ref, en_ref, nu_ref, out_ref,
         sw, et, xt, en, kbuf, pbuf, tbuf, rc, acc, rz, fin, rp,
         swap_s, swap_r, z_s, z_r, p_s, p_r, y_s, y_r, x_s, x_r, en_s, en_r,
         c_s, c_r, rz_s, rz_r, rp_s, rp_r):
    band, pw = lax.axis_index("band"), lax.axis_index("pw")
    z, y_lo, core = lax.div(band, 4), lax.rem(lax.div(band, 2), 2), lax.rem(band, 2)
    y_hi, x = lax.div(pw, 4), lax.rem(pw, 4)
    y = y_hi * 2 + y_lo
    quarter = y_lo * 2 + y_hi

    def dev(xx, yy, zz, cc):
        return ((zz * 2 + lax.rem(yy, 2)) * 2 + cc, lax.div(yy, 2) * 4 + xx)

    def zd(k):
        return dev(x, y, lax.rem(z + k + ZS, ZS), core)

    def yd(k):
        return dev(x, lax.rem(y + k + YS, YS), z, core)

    def xd(k):
        return dev(lax.rem(x + k + XS, XS), y, z, core)

    peer = dev(x, y, z, 1 - core)
    swapper = dev(x, core * 2 + y_lo, z, y_hi)
    swaps = y_hi != core

    def sum_partner(i):
        k, flip = i // 2, i % 2
        return dev(x, y_hi * 2 + lax.rem(y_lo + flip, 2), lax.rem(z + k, ZS), core)

    def pw_partner(i):
        return (band, lax.rem(pw + i, 8))

    barrier = pltpu.get_barrier_semaphore()
    others = [sum_partner(i) for i in range(1, 16)] + [pw_partner(i) for i in range(1, 8)]
    others += [dev(x, lax.rem(y + 3 + 2 * y_lo, YS), z, core), peer]
    for d in others:
        pl.semaphore_signal(barrier, inc=1, device_id=d, device_id_type=MESH)

    @pl.when(swaps)
    def _():
        pl.semaphore_signal(barrier, inc=1, device_id=swapper, device_id_type=MESH)

    for i in range(2):
        en[0, i] = jnp.full((8, 128), en_ref[i], F32)
    pl.semaphore_wait(barrier, len(others) + swaps.astype(jnp.int32))

    def copy(src, dst, ss, rs, d):
        return pltpu.make_async_remote_copy(
            src_ref=src, dst_ref=dst, send_sem=ss, recv_sem=rs, device_id=d, device_id_type=MESH)

    started = []

    def go(c):
        c.start()
        started.append(c)
        return c

    swap_copies = [copy(r, sw.at[0, y_hi, i], swap_s.at[i], swap_r.at[i], swapper)
                   for i, r in enumerate((s_ref, w_ref))]

    zc = {}
    for k in (0, 1, 2):
        zc[k + 1] = copy(sw.at[k, core], sw.at[k + 1, core], z_s.at[k + 1], z_r.at[k + 1], zd(1))
    for k in (0, 7, 6):
        to = (k - 1) % 8
        zc[to] = copy(sw.at[k, core], sw.at[to, core], z_s.at[to], z_r.at[to], zd(-1))
    zc[4] = copy(sw.at[3, core, 0], sw.at[4, core, 0], z_s.at[4], z_r.at[4], zd(1))
    zc[8] = copy(sw.at[5, core, 1], sw.at[4, core, 1], z_s.at[0], z_r.at[0], zd(-1))
    pc = [copy(sw.at[k, core], sw.at[k, core], p_s.at[k], p_r.at[k], peer) for k in range(8)]

    @pl.when(swaps)
    def _():
        for c in swap_copies:
            c.start()

    @pl.when(jnp.logical_not(swaps))
    def _():
        sw[0, core, 0] = s_ref[...]
        sw[0, core, 1] = w_ref[...]
        zc[1].start()
        zc[7].start()
        pc[0].start()

    for q in range(4):
        for b in range(2):
            et[0, q, b] = e_ref[b, q * 128:(q + 1) * 128, :].T

    yc = {
        1: copy(et.at[0], et.at[1], y_s.at[0], y_r.at[0], yd(1)),
        3: copy(et.at[0], et.at[3], y_s.at[1], y_r.at[1], yd(-1)),
        2: copy(et.at[1, pl.ds(0, 2)], et.at[2, pl.ds(0, 2)], y_s.at[2], y_r.at[2], yd(1)),
        4: copy(et.at[3, pl.ds(2, 2)], et.at[2, pl.ds(2, 2)], y_s.at[3], y_r.at[3], yd(-1)),
    }
    enc = copy(en.at[0], en.at[1], en_s, en_r, yd(1))
    xc = {}
    for j in range(4):
        xc[1, j] = copy(et.at[j, quarter], xt.at[1, j], x_s.at[j], x_r.at[j], xd(1))
        xc[3, j] = copy(et.at[j, quarter], xt.at[3, j], x_s.at[4 + j], x_r.at[4 + j], xd(-1))
        if j < 2:
            xc[2, j] = copy(xt.at[1, j], xt.at[2, j], x_s.at[8 + j], x_r.at[8 + j], xd(1))
        else:
            xc[2, j] = copy(xt.at[3, j], xt.at[2, j], x_s.at[8 + j], x_r.at[8 + j], xd(-1))

    go(yc[1])
    go(yc[3])
    go(enc)
    go(xc[1, 0])
    go(xc[3, 0])
    xt[0, 0] = et[0, quarter]

    @pl.when(swaps)
    def _():
        for c in swap_copies:
            c.wait()
        zc[1].start()
        zc[7].start()
        pc[0].start()

    started.extend([zc[1], zc[7], pc[0]])

    nu2 = [nu_ref[e] * nu_ref[e] for e in range(2)]

    def unit(t, p):
        k1 = t
        k2 = 8 - t - 4 * (1 - (t + 3) // 4)
        for bi in range(2):
            eps = en[p, bi, 0:1, :]
            eps = jnp.concatenate([eps, eps], axis=1)
            lhs = []
            for jj in range(2):
                j = p + 2 * jj
                r = lax.div(lax.rem(y - j + YS, YS), 2)
                for h in range(2):
                    rows = pl.ds(h * 256, 256)
                    s = jnp.concatenate([sw[k1, r, 0, rows, :], sw[k2, r, 0, rows, :]], axis=1).astype(F32)
                    w = jnp.concatenate([sw[k1, r, 1, rows, :], sw[k2, r, 1, rows, :]], axis=1).astype(F32)
                    v = w + eps
                    num = s * v
                    sq = v * v
                    for e in range(2):
                        kern = num * pl.reciprocal(sq + nu2[e], approx=True)
                        kbuf[bi, e, pl.ds(jj * 512 + h * 256, 256), :] = kern.astype(BF)
                for q in range(4):
                    lhs.append(et[j, q, bi])
            lhs = jnp.concatenate(lhs, axis=1)
            for e in range(2):
                part = jnp.dot(lhs, kbuf[bi, e], preferred_element_type=F32)
                pbuf[p * 4 + t, bi, e] = part.astype(BF)

    def second(i):
        p, t = lax.div(i, 4), lax.rem(i, 4)
        k1 = t
        k2 = 8 - t - 4 * (1 - (t + 3) // 4)
        group = lax.rem(y_lo + p, 2)

        def place(k):
            zz = lax.rem(z - k + ZS, ZS)
            j = lax.rem(y - (lax.div(zz, 4) * 2 + group) + YS, YS)
            return lax.rem(x - lax.rem(zz, 4) + XS, XS), j

        (i1, j1), (i2, j2) = place(k1), place(k2)
        for e in range(2):
            total = tbuf[e]
            for bi in range(2):
                right = jnp.concatenate([xt[i1, j1, bi], xt[i2, j2, bi]], axis=1)
                total = total + lax.dot_general(
                    pbuf[p * 4 + t, bi, e], right, (((1,), (1,)), ((), ())), preferred_element_type=F32)
            tbuf[e] = total

    def arrived_z(keys):
        for k in keys:
            zc[k].wait_recv()

    arrived_z((1, 7))
    go(zc[2])
    go(zc[6])
    go(pc[1])
    go(pc[7])
    xc[1, 0].wait_recv()
    xc[3, 0].wait_recv()
    go(xc[2, 0])
    arrived_z((2, 6))
    go(zc[3])
    go(zc[5])
    go(pc[2])
    go(pc[6])
    yc[1].wait_recv()
    yc[3].wait_recv()
    go(yc[2])
    go(yc[4])
    for j in (1, 3):
        go(xc[1, j])
        go(xc[3, j])
        xt[0, j] = et[j, quarter]
    enc.wait_recv()
    for k in (1, 7, 2, 6):
        pc[k].wait_recv()

    def first_loop(lo, hi, p):
        def step(t, c):
            unit(t, p)
            return c
        lax.fori_loop(lo, hi, step, 0)

    first_loop(1, 3, 1)
    for j in (1, 3):
        xc[1, j].wait_recv()
        xc[3, j].wait_recv()
    go(xc[2, 1])
    go(xc[2, 3])
    arrived_z((3, 5))
    go(zc[4])
    go(zc[8])
    go(pc[3])
    go(pc[5])
    yc[2].wait_recv()
    yc[4].wait_recv()
    go(xc[1, 2])
    go(xc[3, 2])
    xt[0, 2] = et[2, quarter]
    for k in (3, 5):
        pc[k].wait_recv()

    def mid(i, c):
        over = lax.div(i, 4)
        unit(i - over, over)
        return c

    lax.fori_loop(1, 3, mid, 0)
    arrived_z((4, 8))
    go(pc[4])
    xc[1, 2].wait_recv()
    xc[3, 2].wait_recv()
    go(xc[2, 2])
    lax.fori_loop(3, 5, mid, 0)
    pc[0].wait_recv()
    pc[4].wait_recv()

    def last(p, c):
        unit(0, p)
        return c

    lax.fori_loop(0, 2, last, 0)
    for j in range(4):
        xc[2, j].wait_recv()
    tbuf[...] = jnp.zeros_like(tbuf)

    def second_step(i, c):
        second(i)
        return c

    lax.fori_loop(0, 8, second_step, 0)

    for e in range(2):
        for i in range(16):
            for c in range(2):
                acc[c, i, e] = tbuf[e, (i * 2 + c) * 8:(i * 2 + c + 1) * 8, :] * scale
    cc = go(copy(acc.at[1 - core], rc, c_s, c_r, peer))
    cc.wait_recv()
    rc[...] = rc[...] + acc[core]
    mine = z * 2 + y_lo
    rz_copies = []
    for i in range(1, 16):
        k, flip = i // 2, i % 2
        to = lax.rem(z + k, ZS) * 2 + lax.rem(y_lo + flip, 2)
        rz_copies.append(go(copy(rc.at[to], rz.at[i], rz_s.at[i], rz_r.at[i], sum_partner(i))))
    total = rc[mine]
    for c in rz_copies:
        c.wait_recv()
    for i in range(1, 16):
        total = total + rz[i]
    fin[...] = total
    rp_copies = [go(copy(fin, rp.at[i], rp_s.at[i], rp_r.at[i], pw_partner(i))) for i in range(1, 8)]
    for c in rp_copies:
        c.wait_recv()
    for i in range(1, 8):
        total = total + rp[i]
    out_ref[...] = total
    for c in started:
        c.wait_send()


def on_device(elements, strength, pole_freq, energies, imag_freqs):
    states = elements.shape[2]
    scale = 1.0 / (4096 * math.sqrt(64))
    vm = pl.BlockSpec(memory_space=pltpu.VMEM)
    sm = pl.BlockSpec(memory_space=pltpu.SMEM)
    dma = pltpu.SemaphoreType.DMA
    out = pl.pallas_call(
        lambda *refs: body(scale, *refs),
        out_shape=jax.ShapeDtypeStruct((2, 8, states), F32),
        in_specs=[vm, vm, vm, sm, sm],
        out_specs=vm,
        scratch_shapes=[
            pltpu.VMEM((8, 2, 2, 512, 128), BF),
            pltpu.VMEM((4, 4, 2, 256, 128), BF),
            pltpu.VMEM((4, 4, 2, 256, 128), BF),
            pltpu.VMEM((2, 2, 8, 128), F32),
            pltpu.VMEM((2, 2, 1024, 256), BF),
            pltpu.VMEM((8, 2, 2, 256, 256), BF),
            pltpu.VMEM((2, 256, 256), F32),
            pltpu.VMEM((16, 2, 8, 256), F32),
            pltpu.VMEM((2, 16, 2, 8, 256), F32),
            pltpu.VMEM((16, 2, 8, 256), F32),
            pltpu.VMEM((2, 8, 256), F32),
            pltpu.VMEM((8, 2, 8, 256), F32),
            dma((2,)), dma((2,)),
            dma((8,)), dma((8,)),
            dma((8,)), dma((8,)),
            dma((4,)), dma((4,)),
            dma((12,)), dma((12,)),
            dma, dma,
            dma, dma,
            dma((16,)), dma((16,)),
            dma((8,)), dma((8,)),
        ],
        compiler_params=pltpu.CompilerParams(
            collective_id=0, has_side_effects=True, vmem_limit_bytes=40 * 1024 * 1024),
        cost_estimate=pl.CostEstimate(flops=6_500_000_000, bytes_accessed=1_000_000, transcendentals=8_000_000),
        name="self_energy",
    )(elements, strength, pole_freq, energies, imag_freqs)
    return lax.dynamic_slice_in_dim(out, lax.axis_index("pw") * 32, 32, 2)


def solution(mesh):
    in_specs = (P("band", "pw", None), P("pw", "band"), P("pw", "band"), P("band"), P())
    out_specs = P(None, "band", "pw")
    return jax.shard_map(
        on_device, mesh=mesh, in_specs=in_specs, out_specs=out_specs, check_vma=False
    )
```

time: 1680 us -> 72.6 us (0.04)
  waiting for transfers between devices: 1570 us -> 0 us
  Pallas kernels: 0 us -> 68.2 us
  matrix products: 53.9 us -> 0 us
    reduce_scatter x1 -> x0, waiting for transfers between devices: 1260 us -> none  [on_device(): lax.psum_scatter(blocks, ('band', 'pw'), scatter_dimension=0, tiled=True)[0]]
    ppermute x31 -> x0, waiting for transfers between devices: 231 us -> none  [shifted_2(): return lax.ppermute(value, axis, pairs)]
    all_gather x1 -> x0, waiting for transfers between devices: 76.7 us -> none  [on_device(): whole_rows = lax.all_gather(elements, 'pw', axis=1, tiled=True)]
    pallas_call x0 -> x1, Pallas kernels: none -> 68.2 us  [on_device(): pl.pallas_call(lambda *refs: body(scale, *refs), out_shape=jax.ShapeDtype...]
    dot_general x64 -> x0, matrix products: 53.9 us -> none  [the longest x32 38.2 us: contribute(): jnp.einsum('ebhnc,bcm->enm', partial_value, column_rows, preferred_elemen...]
  transfers between devices with their start and end apart: 33 -> 0, of which waited for: 33 -> 0; matrix products, arithmetic and copies ran while one was open for 0% -> 0% of each run, Pallas kernels for 0% -> 0%
where the time goes in v1:
time: 72.6 us; the launch traced here: 72.4 us
  Pallas kernels  68.2 us (94%)
  local copies, waits for them, and re-layouts  4.2 us (6%)
    pallas_call x1, Pallas kernels, on_device(): pl.pallas_call(lambda *refs: body(scale, *refs), out_shape=jax.ShapeDtype...  68.2 us
    unnamed x10, local copies, waits for them, and re-layouts  3.52 us

profile of v1, /device:TPU:1, one launch (start us, length us, event | category | flops | bytes accessed | tf_op | source)
XLA Modules:
  0.0 72.4 jit_solution(9814227570257960949)
XLA Ops:
  0.0 0.0 copy-start.3
  0.0 0.0 copy-start.4
  0.0 0.7 copy-done.3
  0.7 0.0 copy-done.4
  0.7 0.0 copy-start
  0.7 1.0 %copy-done = bf16[2,512,256]{2,1,0:T(8,128)(2,1)S(1)} copy-done((bf16[2,512,256]{2,1,0:T(8,128)(2,1)S(1)}, bf16[2,512,256]{2,1,0:T(8,128)(2,1)}, u32[]{:S(2)}) %copy-start) | copy-done | bytes 524312
  1.7 0.0 copy-start.1
  1.7 0.9 %copy-done.1 = bf16[512,128]{1,0:T(8,128)(2,1)S(1)} copy-done((bf16[512,128]{1,0:T(8,128)(2,1)S(1)}, bf16[512,128]{1,0:T(8,128)(2,1)}, u32[]{:S(2)}) %copy-start.1) | copy-done | bytes 131096
  2.6 0.0 copy-start.2
  2.6 0.9 %copy-done.2 = bf16[512,128]{1,0:T(8,128)(2,1)S(1)} copy-done((bf16[512,128]{1,0:T(8,128)(2,1)S(1)}, bf16[512,128]{1,0:T(8,128)(2,1)}, u32[]{:S(2)}) %copy-start.2) | copy-done | bytes 131096
  3.5 68.2 %self_energy.1 = f32[2,8,256]{2,1,0:T(8,128)S(1)} custom-call(bf16[2,512,256]{2,1,0:T(8,128)(2,1)S(1)} %copy-done, bf16[512,128]{1,0:T(8,128)(2,1)S(1)} %copy-done.1, bf16[512,128]{1,0:T(8,128)(2,1)S(1)} %copy-done.2, f32[2]{0:T(128)S(1)} %copy-done.3, f32[2]{0:T(128)S(1)} %copy-done.4), custom_call_target="tpu_custom_call" | custom-call | flops 6499999744 | bytes 1000000 | tf_op jit(solution)/shard_map/self_energy/pallas_call | solution.py:305
  71.7 0.7 constant_dynamic-slice_fusion
Async XLA Ops:
  0.0 0.7 copy-start.3
  0.0 0.7 copy-start.4
  0.7 1.0 %copy-start = (bf16[2,512,256]{2,1,0:T(8,128)(2,1)S(1)}, bf16[2,512,256]{2,1,0:T(8,128)(2,1)}, u32[]{:S(2)}) copy-start(bf16[2,512,256]{2,1,0:T(8,128)(2,1)} %refs_0_.1) | copy-start | bytes 1572868
  1.7 0.9 %copy-start.1 = (bf16[512,128]{1,0:T(8,128)(2,1)S(1)}, bf16[512,128]{1,0:T(8,128)(2,1)}, u32[]{:S(2)}) copy-start(bf16[512,128]{1,0:T(8,128)(2,1)} %refs_1_.1) | copy-start | bytes 393220
  2.6 0.9 %copy-start.2 = (bf16[512,128]{1,0:T(8,128)(2,1)S(1)}, bf16[512,128]{1,0:T(8,128)(2,1)}, u32[]{:S(2)}) copy-start(bf16[512,128]{1,0:T(8,128)(2,1)} %refs_2_.1) | copy-start | bytes 393220

commit v2 on v0

v2 whole, which is shorter than its diff:
```python
import math

import jax
import jax.numpy as jnp
from jax import lax
from jax.experimental import pallas as pl
from jax.experimental.pallas import tpu as pltpu
from jax.sharding import PartitionSpec as P

MESH = pl.DeviceIdType.MESH
XS, YS, ZS = 4, 4, 8
BF = jnp.bfloat16
F32 = jnp.float32


def body(scale, e_hbm, s_hbm, w_hbm, en_hbm, nu_hbm, out_ref,
         e_vm, en_sm, nu_sm, sw, et, xt, en, kbuf, pbuf, tbuf, rc, acc, sb, rz, fin, rp,
         in_s, swap_s, swap_r, z_s, z_r, p_s, p_r, y_s, y_r, x_s, x_r, en_s, en_r,
         c_s, c_r, rz_s, rz_r, rp_s, rp_r):
    band, pw = lax.axis_index("band"), lax.axis_index("pw")
    z, y_lo, core = lax.div(band, 4), lax.rem(lax.div(band, 2), 2), lax.rem(band, 2)
    y_hi, x = lax.div(pw, 4), lax.rem(pw, 4)
    y = y_hi * 2 + y_lo

    def quarter_of(k):
        yy = lax.rem(y + k + YS, YS)
        return lax.rem(yy, 2) * 2 + lax.div(yy, 2)

    quarter = quarter_of(0)

    def dev(xx, yy, zz, cc):
        return ((zz * 2 + lax.rem(yy, 2)) * 2 + cc, lax.div(yy, 2) * 4 + xx)

    def zd(k):
        return dev(x, y, lax.rem(z + k + ZS, ZS), core)

    def yd(k):
        return dev(x, lax.rem(y + k + YS, YS), z, core)

    def xd(k):
        return dev(lax.rem(x + k + XS, XS), y, z, core)

    peer = dev(x, y, z, 1 - core)
    swapper = dev(x, core * 2 + y_lo, z, y_hi)
    swaps = y_hi != core
    stays = jnp.logical_not(swaps)

    def sum_partner(i):
        k, flip = i // 2, i % 2
        return dev(x, y_hi * 2 + lax.rem(y_lo + flip, 2), lax.rem(z + k, ZS), core)

    def pw_partner(i):
        return (band, lax.rem(pw + i, 8))

    barrier = pltpu.get_barrier_semaphore()
    others = [sum_partner(i) for i in range(1, 16)] + [pw_partner(i) for i in range(1, 8)]
    others += [dev(x, lax.rem(y + 3 + 2 * y_lo, YS), z, core), peer]
    for d in others:
        pl.semaphore_signal(barrier, inc=1, device_id=d, device_id_type=MESH)

    @pl.when(swaps)
    def _():
        pl.semaphore_signal(barrier, inc=1, device_id=swapper, device_id_type=MESH)

    loads = [pltpu.make_async_copy(e_hbm.at[b], e_vm.at[b], in_s.at[b]) for b in range(2)]
    loads.append(pltpu.make_async_copy(en_hbm, en_sm, in_s.at[2]))
    loads.append(pltpu.make_async_copy(nu_hbm, nu_sm, in_s.at[3]))
    own_loads = [pltpu.make_async_copy(r, sw.at[0, core, i], in_s.at[4 + i]) for i, r in enumerate((s_hbm, w_hbm))]
    for c in loads:
        c.start()

    @pl.when(stays)
    def _():
        for c in own_loads:
            c.start()

    for c in loads:
        c.wait()
    for i in range(2):
        en[0, i] = jnp.full((8, 128), en_sm[i], F32)
    nu2 = [nu_sm[e] * nu_sm[e] for e in range(2)]
    for q in range(4):
        for b in range(2):
            et[0, q, b] = e_vm[b, q * 128:(q + 1) * 128, :].T

    def copy(src, dst, ss, rs, d):
        return pltpu.make_async_remote_copy(
            src_ref=src, dst_ref=dst, send_sem=ss, recv_sem=rs, device_id=d, device_id_type=MESH)

    started = []

    def go(*copies):
        for c in copies:
            c.start()
            started.append(c)

    swap_copies = [copy(r, sw.at[0, y_hi, i], swap_s.at[i], swap_r.at[i], swapper)
                   for i, r in enumerate((s_hbm, w_hbm))]

    zc = {}
    for i in range(2):
        for k in (1, 2, 3) + ((4,) if i == 0 else ()):
            zc[k, i] = copy(sw.at[k - 1, core, i], sw.at[k, core, i], z_s.at[k, i], z_r.at[k, i], zd(1))
        for k in (7, 6, 5) + ((4,) if i == 1 else ()):
            zc[k, i] = copy(sw.at[(k + 1) % 8, core, i], sw.at[k, core, i], z_s.at[k, i], z_r.at[k, i], zd(-1))
    pc = [copy(sw.at[k, core], sw.at[k, core], p_s.at[k], p_r.at[k], peer) for k in range(8)]

    yp, ym = {}, {}
    for a in range(4):
        q = quarter_of(a)
        yp[a] = copy(et.at[0, q], et.at[1, q], y_s.at[0, a], y_r.at[0, a], yd(1))
        ym[a] = copy(et.at[0, q], et.at[3, q], y_s.at[1, a], y_r.at[1, a], yd(-1))
    for a in (2, 0):
        q = quarter_of(a - 1)
        yp[4 + a] = copy(et.at[1, q], et.at[2, q], y_s.at[2, a], y_r.at[2, a], yd(1))
    for a in (3, 1):
        q = quarter_of(a + 1)
        ym[4 + a] = copy(et.at[3, q], et.at[2, q], y_s.at[2, a], y_r.at[2, a], yd(-1))
    enc = copy(en.at[0], en.at[1], en_s, en_r, yd(1))
    xp, xm, xr = {}, {}, {}
    for j in range(4):
        xp[j] = copy(et.at[j, quarter], xt.at[1, j], x_s.at[0, j], x_r.at[0, j], xd(1))
        xm[j] = copy(et.at[j, quarter], xt.at[3, j], x_s.at[1, j], x_r.at[1, j], xd(-1))
        xr[j] = (copy(xt.at[1, j, 0], xt.at[2, j, 0], x_s.at[2, j], x_r.at[2, j], xd(1)),
                 copy(xt.at[3, j, 1], xt.at[2, j, 1], x_s.at[3, j], x_r.at[3, j], xd(-1)))

    def kgen(k):
        t, side = (k, 0) if 0 <= k < 4 else ((8 - k) % 4, 1)

        def chunk(i, c):
            rows = pl.ds(pl.multiple_of(lax.rem(i, 8) * 64, 64), 64)
            s = sw[k, lax.div(i, 8), 0, rows, :].astype(F32)
            w = sw[k, lax.div(i, 8), 1, rows, :].astype(F32)
            to = pl.ds(pl.multiple_of(i * 64, 64), 64)
            for p in range(2):
                for bi in range(2):
                    v = w + en[p, bi, 0:1, :]
                    num = s * v
                    sq = v * v
                    for e in range(2):
                        kern = num * pl.reciprocal(sq + nu2[e], approx=True)
                        kbuf[t, side, p, bi, e, to, :] = kern.astype(BF)
            return c

        lax.fori_loop(0, 16, chunk, 0)

    def first(t, p):
        for bi in range(2):
            lhs = []
            for r in range(2):
                j = lax.rem(y - (r * 2 + lax.rem(y_lo + p, 2)) + YS, YS)
                for q in range(4):
                    lhs.append(et[j, q, bi])
            lhs = jnp.concatenate(lhs, axis=1)
            for e in range(2):
                right = jnp.concatenate([kbuf[t, 0, p, bi, e], kbuf[t, 1, p, bi, e]], axis=1)
                part = jnp.dot(lhs, right, preferred_element_type=F32)
                pbuf[p * 4 + t, bi, e] = part.astype(BF)

    def second(t, p):
        k1 = t
        k2 = 8 - t - 4 * (1 - (t + 3) // 4)
        group = lax.rem(y_lo + p, 2)

        def place(k):
            zz = lax.rem(z - k + ZS, ZS)
            j = lax.rem(y - (lax.div(zz, 4) * 2 + group) + YS, YS)
            return lax.rem(x - lax.rem(zz, 4) + XS, XS), j

        (i1, j1), (i2, j2) = place(k1), place(k2)
        for e in range(2):
            total = tbuf[e]
            for bi in range(2):
                right = jnp.concatenate([xt[i1, j1, bi], xt[i2, j2, bi]], axis=1)
                total = total + lax.dot_general(
                    pbuf[p * 4 + t, bi, e], right, (((1,), (1,)), ((), ())), preferred_element_type=F32)
            tbuf[e] = total

    def loop(f, p, lo, hi):
        def step(t, c):
            f(t, p)
            return c
        lax.fori_loop(lo, hi, step, 0)

    def z_pass(d):
        ks = (d, 8 - d)
        for i in range(2):
            for k in ks:
                zc[k, i].wait_recv()
                to = k + 1 if k == d else k - 1
                if (to, i) in zc and (to != 4 or i == (0 if k == d else 1)):
                    zc[to, i].start()
        for k in ks:
            pc[k].start()

    def own_start(i):
        zc[1, i].start()
        zc[7, i].start()

    pl.semaphore_wait(barrier, len(others) + swaps.astype(jnp.int32))

    @pl.when(swaps)
    def _():
        for c in swap_copies:
            c.start()

    @pl.when(stays)
    def _():
        for i in range(2):
            own_loads[i].wait()
            own_start(i)
        pc[0].start()

    go(enc, yp[2], ym[3], xp[0], xm[0], yp[1], ym[1])
    xt[0, 0] = et[0, quarter]
    tbuf[...] = jnp.zeros_like(tbuf)

    @pl.when(swaps)
    def _():
        for i in range(2):
            swap_copies[i].wait_recv()
            own_start(i)
        pc[0].start()

    @pl.when(stays)
    def _():
        z_pass(1)

    xp[0].wait_recv()
    xm[0].wait_recv()
    go(*xr[0])
    yp[2].wait_recv()
    go(yp[6], yp[0])
    ym[3].wait_recv()
    go(xp[3], xm[3])
    go(ym[7], ym[0])
    enc.wait_recv()

    @pl.when(stays)
    def _():
        z_pass(2)

    @pl.when(swaps)
    def _():
        z_pass(1)

    yp[1].wait_recv()
    go(xp[1], xm[1])
    ym[1].wait_recv()
    go(ym[5], yp[3], ym[2])
    xt[0, 1] = et[1, quarter]
    xt[0, 3] = et[3, quarter]
    pc[0].wait_recv()
    kgen(0)

    yp[6].wait_recv()
    go(xp[2], xm[2])
    xt[0, 2] = et[2, quarter]
    yp[0].wait_recv()
    go(yp[4])

    @pl.when(stays)
    def _():
        z_pass(3)

    @pl.when(swaps)
    def _():
        z_pass(2)

    for j in (3, 1):
        xp[j].wait_recv()
        xm[j].wait_recv()
        go(*xr[j])
    for k in (1, 7):
        pc[k].wait_recv()
        kgen(k)
    yp[3].wait_recv()
    for a in (0, 2):
        ym[a].wait_recv()
    xp[2].wait_recv()
    xm[2].wait_recv()
    go(*xr[2])

    @pl.when(swaps)
    def _():
        z_pass(3)

    loop(first, 1, 1, 2)
    for k in (2, 6):
        pc[k].wait_recv()
        kgen(k)

    @pl.when(stays)
    def _():
        zc[4, 0].wait_recv()
        zc[4, 1].wait_recv()
        pc[4].start()

    loop(first, 1, 2, 3)
    for k in (3, 5):
        pc[k].wait_recv()
        kgen(k)
    yp[4].wait_recv()
    ym[5].wait_recv()
    ym[7].wait_recv()
    loop(first, 0, 1, 4)

    @pl.when(swaps)
    def _():
        zc[4, 0].wait_recv()
        zc[4, 1].wait_recv()
        pc[4].start()

    loop(first, 1, 3, 4)
    for j in range(4):
        for c in xr[j]:
            c.wait_recv()
    loop(second, 0, 1, 4)
    loop(second, 1, 1, 4)
    pc[4].wait_recv()
    kgen(4)
    for p in range(2):
        first(0, p)
        second(0, p)

    for e in range(2):
        for i in range(16):
            for c in range(2):
                acc[c, i, e * 8:(e + 1) * 8, :] = tbuf[e, (i * 2 + c) * 8:(i * 2 + c + 1) * 8, :] * scale
    cc = copy(acc.at[1 - core], rc, c_s, c_r, peer)
    go(cc)
    cc.wait_recv()
    for i in range(16):
        sb[i] = (rc[i] + acc[core, i]).astype(BF)
    mine = z * 2 + y_lo
    rz_copies = []
    for i in range(1, 16):
        k, flip = i // 2, i % 2
        to = lax.rem(z + k, ZS) * 2 + lax.rem(y_lo + flip, 2)
        rz_copies.append(copy(sb.at[to], rz.at[i], rz_s.at[i], rz_r.at[i], sum_partner(i)))
    go(*rz_copies)
    total = rc[mine] + acc[core, mine]
    for c in rz_copies:
        c.wait_recv()
    for i in range(1, 16):
        total = total + rz[i].astype(F32)
    fin[...] = total
    rp_copies = [copy(fin, rp.at[i], rp_s.at[i], rp_r.at[i], pw_partner(i)) for i in range(1, 8)]
    go(*rp_copies)
    for c in rp_copies:
        c.wait_recv()
    for i in range(1, 8):
        total = total + rp[i]
    for e in range(2):
        out_ref[e] = total[e * 8:(e + 1) * 8, :]
    for c in started:
        c.wait_send()
    for c in list(zc.values()) + pc:
        c.wait_send()

    @pl.when(swaps)
    def _():
        for c in swap_copies:
            c.wait_send()


def on_device(elements, strength, pole_freq, energies, imag_freqs):
    states = elements.shape[2]
    scale = 1.0 / (4096 * math.sqrt(64))
    vm = pl.BlockSpec(memory_space=pltpu.VMEM)
    hbm = pl.BlockSpec(memory_space=pltpu.HBM)
    dma = pltpu.SemaphoreType.DMA
    out = pl.pallas_call(
        lambda *refs: body(scale, *refs),
        out_shape=jax.ShapeDtypeStruct((2, 8, states), F32),
        in_specs=[hbm] * 5,
        out_specs=vm,
        scratch_shapes=[
            pltpu.VMEM((2, 512, 256), BF),
            pltpu.SMEM((2,), F32),
            pltpu.SMEM((2,), F32),
            pltpu.VMEM((8, 2, 2, 512, 128), BF),
            pltpu.VMEM((4, 4, 2, 256, 128), BF),
            pltpu.VMEM((4, 4, 2, 256, 128), BF),
            pltpu.VMEM((2, 2, 8, 128), F32),
            pltpu.VMEM((4, 2, 2, 2, 2, 1024, 128), BF),
            pltpu.VMEM((8, 2, 2, 256, 256), BF),
            pltpu.VMEM((2, 256, 256), F32),
            pltpu.VMEM((16, 16, 256), F32),
            pltpu.VMEM((2, 16, 16, 256), F32),
            pltpu.VMEM((16, 16, 256), BF),
            pltpu.VMEM((16, 16, 256), BF),
            pltpu.VMEM((16, 256), F32),
            pltpu.VMEM((8, 16, 256), F32),
            dma((6,)),
            dma((2,)), dma((2,)),
            dma((8, 2)), dma((8, 2)),
            dma((8,)), dma((8,)),
            dma((3, 4)), dma((3, 4)),
            dma((4, 4)), dma((4, 4)),
            dma, dma,
            dma, dma,
            dma((16,)), dma((16,)),
            dma((8,)), dma((8,)),
        ],
        compiler_params=pltpu.CompilerParams(
            collective_id=0, has_side_effects=True, vmem_limit_bytes=63 * 1024 * 1024),
        cost_estimate=pl.CostEstimate(flops=6_500_000_000, bytes_accessed=1_000_000, transcendentals=8_000_000),
        name="self_energy",
    )(elements, strength, pole_freq, energies, imag_freqs)
    return lax.dynamic_slice_in_dim(out, lax.axis_index("pw") * 32, 32, 2)


def solution(mesh):
    in_specs = (P("band", "pw", None), P("pw", "band"), P("pw", "band"), P("band"), P())
    out_specs = P(None, "band", "pw")
    return jax.shard_map(
        on_device, mesh=mesh, in_specs=in_specs, out_specs=out_specs, check_vma=False
    )
```

time: 1680 us -> 61.6 us (0.04)
  waiting for transfers between devices: 1570 us -> 0 us
  Pallas kernels: 0 us -> 60.1 us
  matrix products: 53.9 us -> 0 us
    reduce_scatter x1 -> x0, waiting for transfers between devices: 1260 us -> none  [on_device(): lax.psum_scatter(blocks, ('band', 'pw'), scatter_dimension=0, tiled=True)[0]]
    ppermute x31 -> x0, waiting for transfers between devices: 231 us -> none  [shifted_2(): return lax.ppermute(value, axis, pairs)]
    all_gather x1 -> x0, waiting for transfers between devices: 76.7 us -> none  [on_device(): whole_rows = lax.all_gather(elements, 'pw', axis=1, tiled=True)]
    pallas_call x0 -> x1, Pallas kernels: none -> 60.1 us  [on_device(): pl.pallas_call(lambda *refs: body(scale, *refs), out_shape=jax.ShapeDtype...]
    dot_general x64 -> x0, matrix products: 53.9 us -> none  [the longest x32 38.2 us: contribute(): jnp.einsum('ebhnc,bcm->enm', partial_value, column_rows, preferred_elemen...]
  transfers between devices with their start and end apart: 33 -> 0, of which waited for: 33 -> 0; matrix products, arithmetic and copies ran while one was open for 0% -> 0% of each run, Pallas kernels for 0% -> 0%
where the time goes in v2:
time: 61.6 us; the launch traced here: 61.5 us
  Pallas kernels  60.1 us (98%)
  local copies, waits for them, and re-layouts  1.38 us (2%)
    pallas_call x1, Pallas kernels, on_device(): pl.pallas_call(lambda *refs: body(scale, *refs), out_shape=jax.ShapeDtype...  60.1 us
    dynamic_slice x1, local copies, waits for them, and re-layouts, on_device(): return lax.dynamic_slice_in_dim(out, lax.axis_index('pw') * 32, 32, 2)  1.38 us

profile of v2, /device:TPU:1, one launch (start us, length us, event | category | flops | bytes accessed | tf_op | source)
XLA Modules:
  0.0 61.5 jit_solution(4783185915097884279)
XLA Ops:
  0.0 60.1 %self_energy.1 = f32[2,8,256]{2,1,0:T(8,128)} custom-call(bf16[2,512,256]{2,1,0:T(8,128)(2,1)} %refs_0_.1, bf16[512,128]{1,0:T(8,128)(2,1)} %refs_1_.1, bf16[512,128]{1,0:T(8,128)(2,1)} %refs_2_.1, f32[2]{0:T(128)} %refs_3_.1, f32[2]{0:T(128)} %refs_4_.1), custom_call_target="tpu_custom_call" | custom-call | flops 6499999744 | bytes 1000000 | tf_op jit(solution)/shard_map/self_energy/pallas_call | solution.py:373
  60.1 1.4 %constant_dynamic-slice_fusion = f32[2,8,32]{2,1,0:T(8,128)} fusion(f32[2,8,256]{2,1,0:T(8,128)} %self_energy.1, s32[]{:T(128)S(6)} %select_n.3), kind=kLoop, calls=%fused_computation | loop fusion | bytes 4100 | tf_op jit(solution)/shard_map/dynamic_slice | solution.py:411

commit v3 on v2

v3 whole, which is shorter than its diff:
```python
import math

import jax
import jax.numpy as jnp
from jax import lax
from jax.experimental import pallas as pl
from jax.experimental.pallas import tpu as pltpu
from jax.sharding import PartitionSpec as P

MESH = pl.DeviceIdType.MESH
XS, YS, ZS = 4, 4, 8
BF = jnp.bfloat16
F32 = jnp.float32


def body(scale, e_hbm, s_hbm, w_hbm, en_hbm, nu_hbm, out_ref,
         e_vm, en_sm, nu_sm, sw, et, xt, en, kbuf, pacc, pbuf, tbuf, rc, acc, sb, rz, fin, rp,
         in_s, swap_s, swap_r, z_s, z_r, p_s, p_r, y_s, y_r, x_s, x_r, en_s, en_r,
         c_s, c_r, rz_s, rz_r, rp_s, rp_r, tok):
    band, pw = lax.axis_index("band"), lax.axis_index("pw")
    z, y_lo, core = lax.div(band, 4), lax.rem(lax.div(band, 2), 2), lax.rem(band, 2)
    y_hi, x = lax.div(pw, 4), lax.rem(pw, 4)
    y = y_hi * 2 + y_lo

    def quarter_of(k):
        yy = lax.rem(y + k + YS, YS)
        return lax.rem(yy, 2) * 2 + lax.div(yy, 2)

    quarter = quarter_of(0)

    def dev(xx, yy, zz, cc):
        return ((zz * 2 + lax.rem(yy, 2)) * 2 + cc, lax.div(yy, 2) * 4 + xx)

    def zd(k):
        return dev(x, y, lax.rem(z + k + ZS, ZS), core)

    def yd(k):
        return dev(x, lax.rem(y + k + YS, YS), z, core)

    def xd(k):
        return dev(lax.rem(x + k + XS, XS), y, z, core)

    peer = dev(x, y, z, 1 - core)
    swapper = dev(x, core * 2 + y_lo, z, y_hi)
    swaps = y_hi != core
    stays = jnp.logical_not(swaps)

    def sum_partner(i):
        k, flip = i // 2, i % 2
        return dev(x, y_hi * 2 + lax.rem(y_lo + flip, 2), lax.rem(z + k, ZS), core)

    def pw_partner(i):
        return (band, lax.rem(pw + i, 8))

    barrier = pltpu.get_barrier_semaphore()
    others = [zd(1), zd(-1), yd(1), yd(-1), xd(1), xd(-1), peer]
    for d in others:
        pl.semaphore_signal(barrier, inc=1, device_id=d, device_id_type=MESH)

    @pl.when(swaps)
    def _():
        pl.semaphore_signal(barrier, inc=1, device_id=swapper, device_id_type=MESH)

    loads = [pltpu.make_async_copy(e_hbm.at[b], e_vm.at[b], in_s.at[b]) for b in range(2)]
    loads.append(pltpu.make_async_copy(en_hbm, en_sm, in_s.at[2]))
    loads.append(pltpu.make_async_copy(nu_hbm, nu_sm, in_s.at[3]))
    own_loads = [pltpu.make_async_copy(r, sw.at[0, core, i], in_s.at[4 + i]) for i, r in enumerate((s_hbm, w_hbm))]
    for c in loads:
        c.start()

    @pl.when(stays)
    def _():
        for c in own_loads:
            c.start()

    for c in loads:
        c.wait()
    for i in range(2):
        en[0, i] = jnp.full((8, 128), en_sm[i], F32)
    nu2 = [nu_sm[e] * nu_sm[e] for e in range(2)]
    for q in range(4):
        for b in range(2):
            et[0, q, b] = e_vm[b, q * 128:(q + 1) * 128, :].T

    def copy(src, dst, ss, rs, d):
        return pltpu.make_async_remote_copy(
            src_ref=src, dst_ref=dst, send_sem=ss, recv_sem=rs, device_id=d, device_id_type=MESH)

    started = []

    def go(*copies):
        for c in copies:
            c.start()
            if all(c is not o for o in started):
                started.append(c)

    chunks = [(i, pl.ds(h * 256, 256)) for i in range(2) for h in range(2)]
    own_refs = (s_hbm, w_hbm)
    swap_copies = [copy(own_refs[i].at[rows, :], sw.at[0, y_hi, i, rows, :], swap_s.at[n], swap_r.at[n], swapper)
                   for n, (i, rows) in enumerate(chunks)]

    zc = {}
    for n, (i, rows) in enumerate(chunks):
        for k in (1, 2, 3) + ((4,) if i == 0 else ()):
            zc[k, n] = copy(sw.at[k - 1, core, i, rows, :], sw.at[k, core, i, rows, :], z_s.at[k, n], z_r.at[k, n], zd(1))
        for k in (7, 6, 5) + ((4,) if i == 1 else ()):
            zc[k, n] = copy(sw.at[(k + 1) % 8, core, i, rows, :], sw.at[k, core, i, rows, :], z_s.at[k, n], z_r.at[k, n],
                            zd(-1))
    pc = [copy(sw.at[k, core], sw.at[k, core], p_s.at[k], p_r.at[k], peer) for k in range(8)]

    yp, ym = {}, {}
    for a in range(4):
        q = quarter_of(a)
        yp[a] = copy(et.at[0, q], et.at[1, q], y_s.at[0, a], y_r.at[0, a], yd(1))
        ym[a] = copy(et.at[0, q], et.at[3, q], y_s.at[1, a], y_r.at[1, a], yd(-1))
    for a in (2, 0):
        q = quarter_of(a - 1)
        yp[4 + a] = copy(et.at[1, q], et.at[2, q], y_s.at[2, a], y_r.at[2, a], yd(1))
    for a in (3, 1):
        q = quarter_of(a + 1)
        ym[4 + a] = copy(et.at[3, q], et.at[2, q], y_s.at[2, a], y_r.at[2, a], yd(-1))
    enc = copy(en.at[0], en.at[1], en_s, en_r, yd(1))
    xp, xm, xr = {}, {}, {}
    for j in range(4):
        xp[j] = copy(et.at[j, quarter], xt.at[1, j], x_s.at[0, j], x_r.at[0, j], xd(1))
        xm[j] = copy(et.at[j, quarter], xt.at[3, j], x_s.at[1, j], x_r.at[1, j], xd(-1))
        xr[j] = (copy(xt.at[1, j, 0], xt.at[2, j, 0], x_s.at[2, j], x_r.at[2, j], xd(1)),
                 copy(xt.at[3, j, 1], xt.at[2, j, 1], x_s.at[3, j], x_r.at[3, j], xd(-1)))

    def kgen(k, r):
        t, side = (k, 0) if 0 <= k < 4 else ((8 - k) % 4, 1)

        def chunk(i, c):
            rows = pl.ds(pl.multiple_of(i * 128, 128), 128)
            s = sw[k, r, 0, rows, :].astype(F32)
            w = sw[k, r, 1, rows, :].astype(F32)
            to = pl.ds(pl.multiple_of(r * 512 + i * 128, 128), 128)
            for p in range(2):
                for bi in range(2):
                    v = w + en[p, bi, 0:1, :]
                    num = s * v
                    sq = v * v
                    a0, a1 = sq + nu2[0], sq + nu2[1]
                    both = num * pl.reciprocal(a0 * a1, approx=True)
                    kbuf[t, side, p, bi, 0, to, :] = (both * a1).astype(BF)
                    kbuf[t, side, p, bi, 1, to, :] = (both * a0).astype(BF)
            return c

        lax.fori_loop(0, 4, chunk, 0)

    def pieces(p, part):
        if p == 0:
            return [(2 * part, quarter_of(a), lax.div(lax.rem(y + 2 * part, YS), 2)) for a in range(4)]
        below, above = lax.div(lax.rem(y + 3, YS), 2), lax.div(lax.rem(y + 1, YS), 2)
        if part == 0:
            return [(1, quarter_of(1), below), (1, quarter_of(0), below), (3, quarter_of(0), above), (3, quarter_of(2), above)]
        return [(1, quarter_of(3), below), (1, quarter_of(2), below), (3, quarter_of(1), above), (3, quarter_of(3), above)]

    def block_pieces(p, r):
        j = lax.rem(y - (r * 2 + lax.rem(y_lo + p, 2)) + YS, YS)
        return [(j, q, r) for q in range(4)]

    def product(t, p, some, bi, e):
        left = jnp.concatenate([et[j, q, bi] for j, q, r in some], axis=1)
        right = []
        for j, q, r in some:
            rows = pl.ds(pl.multiple_of(r * 512 + q * 128, 128), 128)
            right.append(jnp.concatenate([kbuf[t, side, p, bi, e, rows, :] for side in range(2)], axis=1))
        return jnp.dot(left, jnp.concatenate(right, axis=0), preferred_element_type=F32)

    def first(t, p, part, some):
        for bi in range(2):
            for e in range(2):
                value = product(t, p, some, bi, e)
                if part == 0:
                    pacc[p * 4 + t, bi, e] = value
                else:
                    pbuf[p * 4 + t, bi, e] = (pacc[p * 4 + t, bi, e] + value).astype(BF)

    def whole(p, lo, hi):
        def step(t, c):
            for bi in range(2):
                for e in range(2):
                    value = product(t, p, pieces(p, 0) + pieces(p, 1), bi, e)
                    pbuf[p * 4 + t, bi, e] = value.astype(BF)
            return c
        lax.fori_loop(lo, hi, step, 0)

    def place(k, p):
        zz = lax.rem(z - k + ZS, ZS)
        j = lax.rem(y - (lax.div(zz, 4) * 2 + lax.rem(y_lo + p, 2)) + YS, YS)
        return lax.rem(x - lax.rem(zz, 4) + XS, XS), j

    def second(ts, ps, fresh, es=(0, 1)):
        for e in es:
            left, right = [], []
            for p in ps:
                for t in ts:
                    (i1, j1), (i2, j2) = place(t, p), place((8 - t) if t else 4, p)
                    for bi in range(2):
                        left.append(pbuf[p * 4 + t, bi, e])
                        right.append(jnp.concatenate([xt[i1, j1, bi], xt[i2, j2, bi]], axis=1))
            value = lax.dot_general(
                jnp.concatenate(left, axis=1), jnp.concatenate(right, axis=1), (((1,), (1,)), ((), ())),
                preferred_element_type=F32)
            tbuf[e] = value if fresh else tbuf[e] + value

    def loop(p, part, lo, hi):
        def step(t, c):
            first(t, p, part, pieces(p, part))
            return c
        lax.fori_loop(lo, hi, step, 0)

    def z_pass(d, ns):
        for n in ns:
            for k, to in ((d, d + 1), (8 - d, 7 - d)):
                zc[k, n].wait_recv()
                if to != 4 or (n < 2) == (k == d):
                    zc[to, n].start()
        if 3 in ns:
            pc[d].start()
            pc[8 - d].start()
            if d > 1:
                token_wait(d - 2)
                token(d - 1)

    def last_tokens():
        token_wait(2)
        token(3, (0,))

    def z_end():
        for n in range(4):
            zc[4, n].wait_recv()
        pc[4].start()

    def own(*ks):
        for k in ks:
            kgen(k, core)

    def other(*ks):
        for k in ks:
            pc[k].wait_recv()
            kgen(k, 1 - core)

    def token(n, ways=(0, 1)):
        for w in ways:
            pl.semaphore_signal(tok.at[w, n], inc=1, device_id=zd(1 - 2 * w), device_id_type=MESH)

    def token_wait(n, ways=(0, 1)):
        for w in ways:
            pl.semaphore_wait(tok.at[w, n], 1)

    def x_on(j):
        xp[j].wait_recv()
        xm[j].wait_recv()
        go(*xr[j])

    def y_one():
        yp[2].wait_recv()
        go(yp[6], yp[0])
        ym[3].wait_recv()
        go(xp[3], xm[3])
        go(ym[7], ym[0])
        token(0)

    def y_two():
        yp[1].wait_recv()
        go(xp[1], xm[1])
        ym[1].wait_recv()
        go(ym[5], yp[3], ym[2])
        xt[0, 1] = et[1, quarter]
        xt[0, 3] = et[3, quarter]

    def y_three():
        yp[6].wait_recv()
        go(xp[2], xm[2])
        xt[0, 2] = et[2, quarter]

    def y_four():
        yp[0].wait_recv()
        go(yp[4])

    def y_five():
        yp[3].wait_recv()
        ym[0].wait_recv()
        ym[2].wait_recv()

    def y_six():
        for c in (yp[4], ym[5], ym[7]):
            c.wait_recv()

    def start():
        go(enc, yp[2], ym[3], xp[0], xm[0], yp[1], ym[1])
        xt[0, 0] = et[0, quarter]

    def finish():
        for j in range(4):
            for c in xr[j]:
                c.wait_recv()
        second((1, 2, 3), (0, 1), True)

    pl.semaphore_wait(barrier, len(others) + swaps.astype(jnp.int32))
    every = range(4)

    @pl.when(stays)
    def _():
        for i in range(2):
            own_loads[i].wait()
        for n in every:
            zc[1, n].start()
            zc[7, n].start()
        pc[0].start()
        start()
        enc.wait_recv()
        own(0)
        z_pass(1, every)
        x_on(0)
        own(1)
        z_pass(2, (0, 1))
        own(7)
        y_one()
        z_pass(2, (2, 3))
        other(0)
        own(2, 6)
        y_two()
        z_pass(3, (0, 1))
        other(1)
        z_pass(3, (2, 3))
        other(7)
        y_three()
        loop(0, 0, 1, 2)
        x_on(3)
        own(3, 5)
        y_four()
        loop(1, 0, 1, 2)
        other(2)
        x_on(1)
        z_end()
        last_tokens()
        other(6)
        loop(0, 0, 2, 3)
        own(4)
        loop(1, 0, 2, 3)
        y_five()
        x_on(2)
        other(3)
        loop(1, 1, 1, 3)
        other(5)
        loop(0, 0, 3, 4)
        whole(1, 3, 4)
        y_six()
        loop(0, 1, 1, 4)
        for p in range(2):
            first(0, p, 0, block_pieces(p, core))
        finish()
        other(4)
        for p in range(2):
            first(0, p, 1, block_pieces(p, 1 - core))

    @pl.when(swaps)
    def _():
        for c in swap_copies:
            c.start()
        start()
        for n in every:
            swap_copies[n].wait_recv()
            zc[1, n].start()
            zc[7, n].start()
        pc[0].start()
        enc.wait_recv()
        x_on(0)
        other(0)
        own(0)
        other(1)
        z_pass(1, (0,))
        y_one()
        z_pass(1, (1, 2, 3))
        own(1)
        y_two()
        own(7)
        other(7)
        z_pass(2, (0, 1))
        loop(0, 0, 1, 2)
        other(2)
        y_three()
        z_pass(2, (2, 3))
        loop(1, 0, 1, 2)
        other(6)
        x_on(3)
        own(2)
        z_pass(3, (0, 1))
        y_four()
        own(6)
        loop(0, 0, 2, 3)
        x_on(1)
        other(3)
        z_pass(3, (2, 3))
        own(3)
        y_five()
        x_on(2)
        last_tokens()
        other(5)
        own(5)
        loop(1, 1, 1, 2)
        loop(0, 0, 3, 4)
        whole(1, 2, 4)
        other(4)
        y_six()
        loop(0, 1, 1, 4)
        for p in range(2):
            first(0, p, 0, block_pieces(p, 1 - core))
        z_end()
        finish()
        own(4)
        for p in range(2):
            first(0, p, 1, block_pieces(p, core))

    core_copies = []
    for e in range(2):
        second((0,), (0, 1), False, (e,))
        for i in range(16):
            for c in range(2):
                acc[c, e, i] = tbuf[e, (i * 2 + c) * 8:(i * 2 + c + 1) * 8, :] * scale
        core_copies.append(copy(acc.at[1 - core, e], rc.at[e], c_s.at[e], c_r.at[e], peer))
        go(core_copies[e])
    token_wait(3, (0,))
    for e in range(2):
        core_copies[e].wait_recv()
    for i in range(16):
        both = jnp.concatenate([rc[e, i] + acc[core, e, i] for e in range(2)], axis=0)
        sb[i] = both.astype(BF)
    mine = z * 2 + y_lo
    rz_copies = []
    for i in range(1, 16):
        k, flip = i // 2, i % 2
        to = lax.rem(z + k, ZS) * 2 + lax.rem(y_lo + flip, 2)
        rz_copies.append(copy(sb.at[to], rz.at[i], rz_s.at[i], rz_r.at[i], sum_partner(i)))
    go(*rz_copies)
    total = jnp.concatenate([rc[e, mine] + acc[core, e, mine] for e in range(2)], axis=0)
    for c in rz_copies:
        c.wait_recv()
    for i in range(1, 16):
        total = total + rz[i].astype(F32)
    fin[...] = total
    rp_copies = [copy(fin, rp.at[i], rp_s.at[i], rp_r.at[i], pw_partner(i)) for i in range(1, 8)]
    go(*rp_copies)
    for c in rp_copies:
        c.wait_recv()
    for i in range(1, 8):
        total = total + rp[i]
    for e in range(2):
        out_ref[e] = total[e * 8:(e + 1) * 8, :]
    for c in started:
        c.wait_send()
    for c in list(zc.values()) + pc:
        c.wait_send()

    @pl.when(swaps)
    def _():
        for c in swap_copies:
            c.wait_send()


def on_device(elements, strength, pole_freq, energies, imag_freqs):
    states = elements.shape[2]
    scale = 1.0 / (4096 * math.sqrt(64))
    vm = pl.BlockSpec(memory_space=pltpu.VMEM)
    hbm = pl.BlockSpec(memory_space=pltpu.HBM)
    dma = pltpu.SemaphoreType.DMA
    out = pl.pallas_call(
        lambda *refs: body(scale, *refs),
        out_shape=jax.ShapeDtypeStruct((2, 8, states), F32),
        in_specs=[hbm] * 5,
        out_specs=vm,
        scratch_shapes=[
            pltpu.VMEM((2, 512, 256), BF),
            pltpu.SMEM((2,), F32),
            pltpu.SMEM((2,), F32),
            pltpu.VMEM((8, 2, 2, 512, 128), BF),
            pltpu.VMEM((4, 4, 2, 256, 128), BF),
            pltpu.VMEM((4, 4, 2, 256, 128), BF),
            pltpu.VMEM((2, 2, 8, 128), F32),
            pltpu.VMEM((4, 2, 2, 2, 2, 1024, 128), BF),
            pltpu.VMEM((8, 2, 2, 256, 256), F32),
            pltpu.VMEM((8, 2, 2, 256, 256), BF),
            pltpu.VMEM((2, 256, 256), F32),
            pltpu.VMEM((2, 16, 8, 256), F32),
            pltpu.VMEM((2, 2, 16, 8, 256), F32),
            pltpu.VMEM((16, 16, 256), BF),
            pltpu.VMEM((16, 16, 256), BF),
            pltpu.VMEM((16, 256), F32),
            pltpu.VMEM((8, 16, 256), F32),
            dma((6,)),
            dma((4,)), dma((4,)),
            dma((8, 4)), dma((8, 4)),
            dma((8,)), dma((8,)),
            dma((3, 4)), dma((3, 4)),
            dma((4, 4)), dma((4, 4)),
            dma, dma,
            dma((2,)), dma((2,)),
            dma((16,)), dma((16,)),
            dma((8,)), dma((8,)),
            pltpu.SemaphoreType.REGULAR((2, 4)),
        ],
        compiler_params=pltpu.CompilerParams(
            collective_id=0, has_side_effects=True, vmem_limit_bytes=63 * 1024 * 1024),
        cost_estimate=pl.CostEstimate(flops=6_500_000_000, bytes_accessed=1_000_000, transcendentals=8_000_000),
        name="self_energy",
    )(elements, strength, pole_freq, energies, imag_freqs)
    return lax.dynamic_slice_in_dim(out, lax.axis_index("pw") * 32, 32, 2)


def solution(mesh):
    in_specs = (P("band", "pw", None), P("pw", "band"), P("pw", "band"), P("band"), P())
    out_specs = P(None, "band", "pw")
    return jax.shard_map(
        on_device, mesh=mesh, in_specs=in_specs, out_specs=out_specs, check_vma=False
    )
```

time: 61.6 us -> 56.6 us (0.919)
  Pallas kernels: 60.1 us -> 54.8 us
    pallas_call x1, Pallas kernels: 60.1 us -> 54.8 us  [on_device(): pl.pallas_call(lambda *refs: body(scale, *refs), out_shape=jax.ShapeDtype...]
where the time goes in v3:
time: 56.6 us; the launch traced here: 56.2 us
  Pallas kernels  54.8 us (97%)
  local copies, waits for them, and re-layouts  1.38 us (2%)
    pallas_call x1, Pallas kernels, on_device(): pl.pallas_call(lambda *refs: body(scale, *refs), out_shape=jax.ShapeDtype...  54.8 us
    dynamic_slice x1, local copies, waits for them, and re-layouts, on_device(): return lax.dynamic_slice_in_dim(out, lax.axis_index('pw') * 32, 32, 2)  1.38 us

profile of v3, /device:TPU:1, one launch (start us, length us, event | category | flops | bytes accessed | tf_op | source)
XLA Modules:
  0.0 56.2 jit_solution(13386283257257653282)
XLA Ops:
  0.0 54.8 %self_energy.1 = f32[2,8,256]{2,1,0:T(8,128)} custom-call(bf16[2,512,256]{2,1,0:T(8,128)(2,1)} %refs_0_.1, bf16[512,128]{1,0:T(8,128)(2,1)} %refs_1_.1, bf16[512,128]{1,0:T(8,128)(2,1)} %refs_2_.1, f32[2]{0:T(128)} %refs_3_.1, f32[2]{0:T(128)} %refs_4_.1), custom_call_target="tpu_custom_call" | custom-call | flops 6499999744 | bytes 1000000 | tf_op jit(solution)/shard_map/self_energy/pallas_call | solution.py:470
  54.8 1.4 %constant_dynamic-slice_fusion = f32[2,8,32]{2,1,0:T(8,128)} fusion(f32[2,8,256]{2,1,0:T(8,128)} %self_energy.1, s32[]{:T(128)S(6)} %select_n.3), kind=kLoop, calls=%fused_computation | loop fusion | bytes 4100 | tf_op jit(solution)/shard_map/dynamic_slice | solution.py:510

commit v4 on v3

--- a/solution.py
+++ b/solution.py
@@ -431,7 +431,8 @@
         sb[i] = both.astype(BF)
     mine = z * 2 + y_lo
     rz_copies = []
-    for i in range(1, 16):
+    far_first = sorted(range(1, 16), key=lambda i: -(min(i // 2, ZS - i // 2) + i % 2))
+    for i in far_first:
         k, flip = i // 2, i % 2
         to = lax.rem(z + k, ZS) * 2 + lax.rem(y_lo + flip, 2)
         rz_copies.append(copy(sb.at[to], rz.at[i], rz_s.at[i], rz_r.at[i], sum_partner(i)))
@@ -441,11 +442,14 @@
         c.wait_recv()
     for i in range(1, 16):
         total = total + rz[i].astype(F32)
-    fin[...] = total
-    rp_copies = [copy(fin, rp.at[i], rp_s.at[i], rp_r.at[i], pw_partner(i)) for i in range(1, 8)]
+    for half in range(2):
+        fin[half] = total[:, half * 128:(half + 1) * 128]
+    rp_copies = [copy(fin.at[lax.div(lax.rem(pw + i, 8), 4)], rp.at[i], rp_s.at[i], rp_r.at[i], pw_partner(i))
+                 for i in (6, 2, 5, 3, 7, 1, 4)]
     go(*rp_copies)
     for c in rp_copies:
         c.wait_recv()
+    total = fin[y_hi]
     for i in range(1, 8):
         total = total + rp[i]
     for e in range(2):
@@ -462,14 +466,13 @@
 
 
 def on_device(elements, strength, pole_freq, energies, imag_freqs):
-    states = elements.shape[2]
     scale = 1.0 / (4096 * math.sqrt(64))
     vm = pl.BlockSpec(memory_space=pltpu.VMEM)
     hbm = pl.BlockSpec(memory_space=pltpu.HBM)
     dma = pltpu.SemaphoreType.DMA
     out = pl.pallas_call(
         lambda *refs: body(scale, *refs),
-        out_shape=jax.ShapeDtypeStruct((2, 8, states), F32),
+        out_shape=jax.ShapeDtypeStruct((2, 8, 128), F32),
         in_specs=[hbm] * 5,
         out_specs=vm,
         scratch_shapes=[
@@ -488,8 +491,8 @@
             pltpu.VMEM((2, 2, 16, 8, 256), F32),
             pltpu.VMEM((16, 16, 256), BF),
             pltpu.VMEM((16, 16, 256), BF),
-            pltpu.VMEM((16, 256), F32),
-            pltpu.VMEM((8, 16, 256), F32),
+            pltpu.VMEM((2, 16, 128), F32),
+            pltpu.VMEM((8, 16, 128), F32),
             dma((6,)),
             dma((4,)), dma((4,)),
             dma((8, 4)), dma((8, 4)),
@@ -507,7 +510,7 @@
         cost_estimate=pl.CostEstimate(flops=6_500_000_000, bytes_accessed=1_000_000, transcendentals=8_000_000),
         name="self_energy",
     )(elements, strength, pole_freq, energies, imag_freqs)
-    return lax.dynamic_slice_in_dim(out, lax.axis_index("pw") * 32, 32, 2)
+    return lax.dynamic_slice_in_dim(out, lax.rem(lax.axis_index("pw"), 4) * 32, 32, 2)
 
 
 def solution(mesh):

time: 56.6 us -> 55.6 us (0.982)
  Pallas kernels: 54.8 us -> 53.8 us
    pallas_call x1, Pallas kernels: 54.8 us -> 53.8 us  [on_device(): pl.pallas_call(lambda *refs: body(scale, *refs), out_shape=jax.ShapeDtype...]
where the time goes in v4:
time: 55.6 us; the launch traced here: 55.2 us
  Pallas kernels  53.8 us (97%)
  local copies, waits for them, and re-layouts  1.37 us (2%)
    pallas_call x1, Pallas kernels, on_device(): pl.pallas_call(lambda *refs: body(scale, *refs), out_shape=jax.ShapeDtype...  53.8 us
    dynamic_slice x1, local copies, waits for them, and re-layouts, on_device(): lax.dynamic_slice_in_dim(out, lax.rem(lax.axis_index('pw'), 4) * 32, 32, 2)  1.37 us

profile of v4, /device:TPU:1, one launch (start us, length us, event | category | flops | bytes accessed | tf_op | source)
XLA Modules:
  0.0 55.2 jit_solution(1258454884093088501)
XLA Ops:
  0.0 53.8 %self_energy.1 = f32[2,8,128]{2,1,0:T(8,128)} custom-call(bf16[2,512,256]{2,1,0:T(8,128)(2,1)} %refs_0_.1, bf16[512,128]{1,0:T(8,128)(2,1)} %refs_1_.1, bf16[512,128]{1,0:T(8,128)(2,1)} %refs_2_.1, f32[2]{0:T(128)} %refs_3_.1, f32[2]{0:T(128)} %refs_4_.1), custom_call_target="tpu_custom_call" | custom-call | flops 6499999744 | bytes 1000000 | tf_op jit(solution)/shard_map/self_energy/pallas_call | solution.py:473
  53.8 1.4 %constant_dynamic-slice_fusion = f32[2,8,32]{2,1,0:T(8,128)} fusion(f32[2,8,128]{2,1,0:T(8,128)} %self_energy.1, s32[]{:T(128)S(6)} %select_n.3), kind=kLoop, calls=%fused_computation | loop fusion | bytes 4100 | tf_op jit(solution)/shard_map/dynamic_slice | solution.py:513

commit v5 on v4

--- a/solution.py
+++ b/solution.py
@@ -160,18 +160,21 @@
         j = lax.rem(y - (r * 2 + lax.rem(y_lo + p, 2)) + YS, YS)
         return [(j, q, r) for q in range(4)]
 
-    def product(t, p, some, bi, e):
+    def product(t, p, some, bi):
         left = jnp.concatenate([et[j, q, bi] for j, q, r in some], axis=1)
         right = []
         for j, q, r in some:
             rows = pl.ds(pl.multiple_of(r * 512 + q * 128, 128), 128)
-            right.append(jnp.concatenate([kbuf[t, side, p, bi, e, rows, :] for side in range(2)], axis=1))
-        return jnp.dot(left, jnp.concatenate(right, axis=0), preferred_element_type=F32)
+            right.append(jnp.concatenate(
+                [kbuf[t, side, p, bi, e, rows, :] for e in range(2) for side in range(2)], axis=1))
+        value = jnp.dot(left, jnp.concatenate(right, axis=0), preferred_element_type=F32)
+        return value[:, :256], value[:, 256:]
 
     def first(t, p, part, some):
         for bi in range(2):
+            values = product(t, p, some, bi)
             for e in range(2):
-                value = product(t, p, some, bi, e)
+                value = values[e]
                 if part == 0:
                     pacc[p * 4 + t, bi, e] = value
                 else:
@@ -180,11 +183,11 @@
     def whole(p, lo, hi):
         def step(t, c):
             for bi in range(2):
+                values = product(t, p, pieces(p, 0) + pieces(p, 1), bi)
                 for e in range(2):
-                    value = product(t, p, pieces(p, 0) + pieces(p, 1), bi, e)
-                    pbuf[p * 4 + t, bi, e] = value.astype(BF)
+                    pbuf[p * 4 + t, bi, e] = values[e].astype(BF)
             return c
-        lax.fori_loop(lo, hi, step, 0)
+        lax.fori_loop(lo, hi, step, 0, unroll=True)
 
     def place(k, p):
         zz = lax.rem(z - k + ZS, ZS)
@@ -209,7 +212,7 @@
         def step(t, c):
             first(t, p, part, pieces(p, part))
             return c
-        lax.fori_loop(lo, hi, step, 0)
+        lax.fori_loop(lo, hi, step, 0, unroll=True)
 
     def z_pass(d, ns):
         for n in ns:
@@ -436,7 +439,16 @@
         k, flip = i // 2, i % 2
         to = lax.rem(z + k, ZS) * 2 + lax.rem(y_lo + flip, 2)
         rz_copies.append(copy(sb.at[to], rz.at[i], rz_s.at[i], rz_r.at[i], sum_partner(i)))
+    sent = list(started)
     go(*rz_copies)
+    for c in sent + list(zc.values()) + pc:
+        c.wait_send()
+
+    @pl.when(swaps)
+    def _():
+        for c in swap_copies:
+            c.wait_send()
+
     total = jnp.concatenate([rc[e, mine] + acc[core, e, mine] for e in range(2)], axis=0)
     for c in rz_copies:
         c.wait_recv()
@@ -447,6 +459,8 @@
     rp_copies = [copy(fin.at[lax.div(lax.rem(pw + i, 8), 4)], rp.at[i], rp_s.at[i], rp_r.at[i], pw_partner(i))
                  for i in (6, 2, 5, 3, 7, 1, 4)]
     go(*rp_copies)
+    for c in rz_copies:
+        c.wait_send()
     for c in rp_copies:
         c.wait_recv()
     total = fin[y_hi]
@@ -454,15 +468,8 @@
         total = total + rp[i]
     for e in range(2):
         out_ref[e] = total[e * 8:(e + 1) * 8, :]
-    for c in started:
+    for c in rp_copies:
         c.wait_send()
-    for c in list(zc.values()) + pc:
-        c.wait_send()
-
-    @pl.when(swaps)
-    def _():
-        for c in swap_copies:
-            c.wait_send()
 
 
 def on_device(elements, strength, pole_freq, energies, imag_freqs):

time: 55.6 us -> 54.6 us (0.982)
  Pallas kernels: 53.8 us -> 52.8 us
    pallas_call x1, Pallas kernels: 53.8 us -> 52.8 us  [on_device(): pl.pallas_call(lambda *refs: body(scale, *refs), out_shape=jax.ShapeDtype...]
where the time goes in v5:
time: 54.6 us; the launch traced here: 54.2 us
  Pallas kernels  52.8 us (97%)
  local copies, waits for them, and re-layouts  1.37 us (3%)
    pallas_call x1, Pallas kernels, on_device(): pl.pallas_call(lambda *refs: body(scale, *refs), out_shape=jax.ShapeDtype...  52.8 us
    dynamic_slice x1, local copies, waits for them, and re-layouts, on_device(): lax.dynamic_slice_in_dim(out, lax.rem(lax.axis_index('pw'), 4) * 32, 32, 2)  1.37 us

profile of v5, /device:TPU:1, one launch (start us, length us, event | category | flops | bytes accessed | tf_op | source)
XLA Modules:
  0.0 54.2 jit_solution(2587527479836632824)
XLA Ops:
  0.0 52.8 %self_energy.1 = f32[2,8,128]{2,1,0:T(8,128)} custom-call(bf16[2,512,256]{2,1,0:T(8,128)(2,1)} %refs_0_.1, bf16[512,128]{1,0:T(8,128)(2,1)} %refs_1_.1, bf16[512,128]{1,0:T(8,128)(2,1)} %refs_2_.1, f32[2]{0:T(128)} %refs_3_.1, f32[2]{0:T(128)} %refs_4_.1), custom_call_target="tpu_custom_call" | custom-call | flops 6499999744 | bytes 1000000 | tf_op jit(solution)/shard_map/self_energy/pallas_call | solution.py:480
  52.8 1.4 %constant_dynamic-slice_fusion = f32[2,8,32]{2,1,0:T(8,128)} fusion(f32[2,8,128]{2,1,0:T(8,128)} %self_energy.1, s32[]{:T(128)S(6)} %select_n.3), kind=kLoop, calls=%fused_computation | loop fusion | bytes 4100 | tf_op jit(solution)/shard_map/dynamic_slice | solution.py:520

commit v6 on v5

--- a/solution.py
+++ b/solution.py
@@ -410,9 +410,9 @@
         other(4)
         y_six()
         loop(0, 1, 1, 4)
+        z_end()
         for p in range(2):
             first(0, p, 0, block_pieces(p, 1 - core))
-        z_end()
         finish()
         own(4)
         for p in range(2):

time: 54.6 us -> 55.5 us (1.016)
  Pallas kernels: 52.8 us -> 53.9 us
    pallas_call x1, Pallas kernels: 52.8 us -> 53.9 us  [on_device(): pl.pallas_call(lambda *refs: body(scale, *refs), out_shape=jax.ShapeDtype...]
where the time goes in v6:
time: 55.5 us; the launch traced here: 55.3 us
  Pallas kernels  53.9 us (97%)
  local copies, waits for them, and re-layouts  1.37 us (2%)
    pallas_call x1, Pallas kernels, on_device(): pl.pallas_call(lambda *refs: body(scale, *refs), out_shape=jax.ShapeDtype...  53.9 us
    dynamic_slice x1, local copies, waits for them, and re-layouts, on_device(): lax.dynamic_slice_in_dim(out, lax.rem(lax.axis_index('pw'), 4) * 32, 32, 2)  1.37 us

profile of v6, /device:TPU:1, one launch (start us, length us, event | category | flops | bytes accessed | tf_op | source)
XLA Modules:
  0.0 55.3 jit_solution(15945724662507621797)
XLA Ops:
  0.0 53.9 %self_energy.1 = f32[2,8,128]{2,1,0:T(8,128)} custom-call(bf16[2,512,256]{2,1,0:T(8,128)(2,1)} %refs_0_.1, bf16[512,128]{1,0:T(8,128)(2,1)} %refs_1_.1, bf16[512,128]{1,0:T(8,128)(2,1)} %refs_2_.1, f32[2]{0:T(128)} %refs_3_.1, f32[2]{0:T(128)} %refs_4_.1), custom_call_target="tpu_custom_call" | custom-call | flops 6499999744 | bytes 1000000 | tf_op jit(solution)/shard_map/self_energy/pallas_call | solution.py:480
  53.9 1.4 %constant_dynamic-slice_fusion = f32[2,8,32]{2,1,0:T(8,128)} fusion(f32[2,8,128]{2,1,0:T(8,128)} %self_energy.1, s32[]{:T(128)S(6)} %select_n.3), kind=kLoop, calls=%fused_computation | loop fusion | bytes 4100 | tf_op jit(solution)/shard_map/dynamic_slice | solution.py:520
